TPU v7x, 128 devices: a whole 4x4x4 slice. The times are simulated.
128 devices in a mesh: mp: 8 (over z, x_lo), dp: 16 (over x_hi, y, core).
Axes of the slice: x: 4 (x_hi: 2, x_lo: 2; x = x_hi * 2 + x_lo), y: 4, z: 4, core: 2. Of those that a mesh axis runs over, the one named last changes fastest.
Arguments:
- volume: bfloat16 [16, 64, 64, 2048], P('dp', 'mp'), may hold values from -6 to 6
- kernel_a: bfloat16 [3, 3, 3, 32, 64], replicated, may hold values from -0.21875 to 0.21875
- kernel_b: bfloat16 [3, 3, 3, 64, 128], P(None, None, None, 'mp'), may hold values from -0.15625 to 0.15625
- cotangent: bfloat16 [16, 16, 16, 16, 128], P('dp', None, None, None, 'mp'), may hold values from -6 to 6
Outputs:
- features: bfloat16 [16, 16, 16, 16, 128], P('dp', None, None, None, 'mp')
- grad_a: float32 [3, 3, 3, 32, 64], replicated
- grad_b: float32 [3, 3, 3, 64, 128], P(None, None, None, 'mp')
All inputs are finite; a program needn't handle non-finite values.
Results may differ from a plain program's by a relative error of at most 0.0049.
Values may be sent and summed in bfloat16 or wider, within the bound.
A program may use at most 192 MiB of HBM per device.

v0:
```python
import math
import jax
import jax.numpy as jnp
from jax import lax
from jax.sharding import PartitionSpec as P

GRID = 64


def shifted(array, axis, by):
    size = lax.axis_size(axis)
    pairs = [(i, i + by) for i in range(size) if 0 <= i + by < size]
    return lax.ppermute(array, axis, pairs)


def forward_conv(padded, kernel):
    return lax.conv_general_dilated(
        padded,
        kernel,
        (2, 2, 2),
        "VALID",
        dimension_numbers=("NDHWC", "DHWIO", "NDHWC"),
        preferred_element_type=jnp.float32,
    )


def kernel_grad(padded, grads):
    result = lax.conv_general_dilated(
        padded,
        grads,
        (1, 1, 1),
        "VALID",
        rhs_dilation=(2, 2, 2),
        dimension_numbers=("CDHWN", "IDHWO", "NDHWC"),
        preferred_element_type=jnp.float32,
    )
    return jnp.transpose(result, (1, 2, 3, 0, 4))


def input_grad(grads, kernel, first_low):
    flipped = kernel[::-1, ::-1, ::-1]
    return lax.conv_general_dilated(
        grads,
        flipped,
        (1, 1, 1),
        ((first_low, 2), (1, 2), (1, 2)),
        lhs_dilation=(2, 2, 2),
        dimension_numbers=("NDHWC", "DHWOI", "NDHWC"),
        preferred_element_type=jnp.float32,
    )


def pad_sides(field):
    return jnp.pad(field, ((0, 0), (0, 0), (1, 0), (1, 0), (0, 0)))


def pad_low(field):
    return jnp.pad(field, ((0, 0), (1, 0), (1, 0), (1, 0), (0, 0)))


def shards(volume, kernel_a, kernel_b, cotangent):
    samp_local = volume.shape[0]
    planes = volume.shape[1]
    edge = volume.shape[2]
    in_chan = kernel_a.shape[3]
    field = volume.reshape(samp_local, planes, edge, edge, in_chan)
    below = shifted(field[:, planes - 1 :], "mp", 1)
    padded_x = pad_sides(jnp.concatenate([below, field], axis=1))
    pre = forward_conv(padded_x, kernel_a)
    hidden = jnp.where(pre > 0, pre, 0.3 * pre).astype(jnp.bfloat16)
    grouped = lax.all_to_all(hidden, "mp", split_axis=4, concat_axis=1, tiled=True)
    padded_h = pad_low(grouped)
    partial_out = forward_conv(padded_h, kernel_b)
    features = lax.psum_scatter(partial_out, "mp", scatter_dimension=4, tiled=True).astype(
        jnp.bfloat16
    )
    upstream = lax.all_gather(cotangent, "mp", axis=4, tiled=True)
    local_b = kernel_grad(padded_h, upstream)
    back_group = input_grad(upstream, kernel_b, 1).astype(jnp.bfloat16)
    back = lax.all_to_all(back_group, "mp", split_axis=1, concat_axis=4, tiled=True)
    delta = (back.astype(jnp.float32) * jnp.where(pre > 0, 1.0, 0.3)).astype(jnp.bfloat16)
    local_a = kernel_grad(padded_x, delta)
    total_a = lax.psum(local_a, ("mp", "dp"))
    total_b = lax.psum(local_b, "dp")
    samples_all = samp_local * lax.axis_size("dp")
    grad_a = total_a / math.sqrt(samples_all * (GRID // 2) ** 3)
    grad_b = total_b / math.sqrt(samples_all * (GRID // 4) ** 3)
    return (features, grad_a, grad_b)


def solution(mesh):
    return jax.shard_map(
        shards,
        mesh=mesh,
        in_specs=(
            P("dp", "mp", None, None),
            P(),
            P(None, None, None, "mp", None),
            P("dp", None, None, None, "mp"),
        ),
        out_specs=(P("dp", None, None, None, "mp"), P(), P(None, None, None, "mp", None)),
        check_vma=False,
    )
```

profile of v0, /device:TPU:1, one launch (start us, length us, event | category | flops | bytes accessed | tf_op | source)
XLA Modules:
  0.0 838.3 jit_solution(7763710412680146833)
XLA Ops:
  7.2 4.9 copy.124
  14.2 4.0 collective-permute-start
  18.2 31.5 %copy.127 = bf16[1,8,64,64,32]{4,0,3,2,1:T(2,128)(2,1)} copy(bf16[1,8,64,64,32]{2,4,3,1,0:T(8,128)(2,1)} %bitcast.69) | data formatting | bytes 4194304 | tf_op jit(solution)/shard_map/reshape | solution.py:66
  52.4 58.2 %pad_maximum_fusion = bf16[1,9,64,64,32]{4,0,3,2,1:T(2,128)(2,1)} fusion(bf16[1,8,64,64,32]{4,0,3,2,1:T(2,128)(2,1)} %copy.127, bf16[1,1,64,64,32]{4,0,3,2,1:T(2,128)(2,1)S(1)} %copy.126), kind=kLoop, calls=%fused_computation.4 | loop fusion | flops 1179648 | bytes 4718592 | tf_op jit(solution)/shard_map/concatenate | solution.py:68
  110.6 33.5 %copy.128 = bf16[1,9,64,64,32]{3,4,2,1,0:T(8,128)(2,1)} copy(bf16[1,9,64,64,32]{4,0,3,2,1:T(2,128)(2,1)} %pad_maximum_fusion) | data formatting | bytes 4718592 | tf_op jit(solution)/shard_map/concatenate | solution.py:68
  144.1 9.2 %copy.159 = bf16[9,64,1,64,32]{1,4,3,0,2:T(8,128)(2,1)} copy(bf16[9,64,1,64,32]{3,4,2,1,0:T(8,128)(2,1)} %bitcast.72) | data formatting | bytes 4718592
  153.3 6.1 pad.4.clone
  159.4 15.6 %copy.131 = bf16[9,64,1,8,10,32]{5,3,4,1,0,2:T(8,128)(2,1)} copy(bf16[9,64,1,8,10,32]{1,5,4,3,0,2:T(8,128)(2,1)} %bitcast.67) | data formatting | bytes 5898240 | tf_op jit(solution)/shard_map/conv_general_dilated | solution.py:17
  177.4 12.0 %compare_select_fusion = (f32[4,32,8,5,64]{4,2,3,1,0:T(8,128)}, bf16[4,32,8,5,64]{4,2,3,1,0:T(8,128)(2,1)S(1)}) fusion(pred[8,5]{0,1:T(8,128)(4,1)S(1)} %copy-done.6, bf16[3,3,3,32,64]{4,3,2,1,0:T(8,128)(2,1)S(1)} %copy-done, bf16[9,64,1,7,2,32]{5,3,4,1,0,2:T(8,128)(2,1)S(1)} %slice.12, bf16[9,64,1,8,10,32]{5,3,4,1,0,2:T(8,128)(2,1)} %copy.131), kind=kOutput, calls=%fused_computation.20 | convolution fusion | flops 572915712 | bytes 5541928 | tf_op jit(solution)/shard_map/conv_general_dilated | solution.py:17
  195.8 6.1 all-to-all-start
  202.0 3.9 copy.140
  216.9 3.4 copy.160
  220.4 4.0 pad.6.clone
  224.4 12.8 %copy.138 = bf16[32,32,1,8,6,8]{5,3,4,1,0,2:T(8,128)(2,1)} copy(bf16[32,32,1,8,6,8]{1,5,4,3,0,2:T(8,128)(2,1)} %bitcast.73) | data formatting | bytes 1572864 | tf_op jit(solution)/shard_map/conv_general_dilated | solution.py:17
  240.6 12.3 %broadcast_select_fusion = f32[16,16,8,3,128]{4,2,3,1,0:T(8,128)S(1)} fusion(pred[8,3]{0,1:T(4,128)(4,1)S(1)} %copy-done.7, bf16[3,3,3,8,128]{4,3,2,1,0:T(8,128)(2,1)S(1)} %copy-done.5, bf16[32,32,1,7,2,8]{5,3,4,1,0,2:T(8,128)(2,1)S(1)} %slice.14, bf16[32,32,1,8,6,8]{5,3,4,1,0,2:T(8,128)(2,1)} %copy.138), kind=kOutput, calls=%fused_computation.30 | convolution fusion | flops 329662464 | bytes 4216856 | tf_op jit(solution)/shard_map/conv_general_dilated | solution.py:17
  255.2 23.8 %copy.153 = bf16[1,32,32,32,8]{4,0,3,2,1:T(2,128)(2,1)} copy(bf16[1,32,32,32,8]{3,4,2,1,0:T(8,128)(2,1)S(1)} %bitcast.71) | data formatting | bytes 1048576 | tf_op jit(solution)/shard_map/all_to_all | solution.py:71
  279.0 97.7 %all-gather.2.cloned.1.call-done = bf16[1,16,16,16,128]{3,2,1,0,4:T(8,128)(2,1)} async-done(((bf16[1,16,16,16,16]{3,2,1,0,4:T(8,128)(2,1)}), bf16[1,16,16,16,128]{3,2,1,0,4:T(8,128)(2,1)}) %all-gather.2.cloned.1.call-update) | async-done | bytes 1048592 | tf_op jit(solution)/shard_map/all_gather | solution.py:77
  376.7 10.0 %copy.141 = bf16[1,16,16,16,128]{4,3,2,1,0:T(8,128)(2,1)S(1)} copy(bf16[1,16,16,16,128]{3,2,1,0,4:T(8,128)(2,1)} %all-gather.2.cloned.1.call-done) | data formatting | bytes 2097152 | tf_op jit(solution)/shard_map/all_gather | solution.py:77
  387.9 14.3 %fusion.17 = bf16[32,32,8,6,8]{4,2,3,1,0:T(8,128)(2,1)} fusion(bf16[3,3,3,8,128]{4,3,2,1,0:T(8,128)(2,1)S(1)} %copy-done.5, bf16[16,16,1,7,1,128]{5,3,4,1,0,2:T(8,128)(2,1)S(1)} %slice.16, bf16[16,16,1,8,3,128]{5,3,4,1,0,2:T(8,128)(2,1)S(1)} %copy.144), kind=kOutput, calls=%fused_computation.24 | convolution fusion | flops 332021760 | bytes 2873344 | tf_op jit(solution)/shard_map/conv_general_dilated | solution.py:42
  402.2 13.6 %copy.145 = bf16[32,32,8,6,8]{1,4,3,2,0:T(8,128)(2,1)S(1)} copy(bf16[32,32,8,6,8]{4,2,3,1,0:T(8,128)(2,1)} %fusion.17) | data formatting | bytes 1572864 | tf_op jit(solution)/shard_map/conv_general_dilated | solution.py:42
  419.7 4.9 all-to-all-start.1
  424.6 13.5 %copy.154 = bf16[1,16,16,16,128]{4,0,3,2,1:T(2,128)(2,1)S(1)} copy(bf16[1,16,16,16,128]{3,2,1,0,4:T(8,128)(2,1)} %all-gather.2.cloned.1.call-done) | data formatting | bytes 2097152 | tf_op jit(solution)/shard_map/all_gather | solution.py:77
  438.1 51.8 %fusion.36 = f32[3,3,3,8,128]{4,3,2,1,0:T(8,128)} fusion(bf16[1,32,32,32,8]{4,0,3,2,1:T(2,128)(2,1)} %copy.153, bf16[1,16,16,16,128]{4,0,3,2,1:T(2,128)(2,1)S(1)} %copy.154), kind=kOutput, calls=%fused_computation.46 | convolution fusion | flops 212629504 | bytes 1683456 | tf_op jit(solution)/shard_map/transpose | solution.py:37
  491.3 3.4 copy.147
  494.7 3.5 fusion.12
  498.2 4.1 copy.151
  502.3 46.6 %fusion.35 = f32[3,3,3,32,64]{4,3,2,1,0:T(8,128)} fusion(bf16[1,9,64,64,32]{4,0,3,2,1:T(2,128)(2,1)} %pad_maximum_fusion, bf16[1,4,32,32,64]{4,0,3,2,1:T(2,128)(2,1)} %copy.151), kind=kOutput, calls=%fused_computation.45 | convolution fusion | flops 443596800 | bytes 3104768 | tf_op jit(solution)/shard_map/transpose | solution.py:37
  550.5 14.3 %copy.156 = f32[1,16,16,16,128]{2,3,1,0,4:T(8,128)} copy(f32[1,16,16,16,128]{4,2,3,1,0:T(8,128)} %slice_bitcast_fusion.1) | data formatting | bytes 4194304
  564.8 15.3 %reshape.69 = f32[128,4096]{1,0:T(8,128)} reshape(f32[128,1,16,16,16]{4,3,2,1,0:T(8,128)} %bitcast.66) | data formatting | bytes 4194304
  580.1 45.1 %all-reduce.5.cloned.1.call-done = f32[3,3,3,8,128]{4,3,2,1,0:T(8,128)} async-done(((f32[3,3,3,8,128]{4,3,2,1,0:T(8,128)}), f32[3,3,3,8,128]{4,3,2,1,0:T(8,128)}) %all-reduce.5.cloned.1.call-update) | async-done | bytes 110608 | tf_op jit(solution)/shard_map/psum | solution.py:84
  626.8 147.3 %all-reduce.3.cloned.1.call-done = f32[3,3,3,32,64]{4,3,2,1,0:T(8,128)} async-done(((f32[3,3,3,32,64]{4,3,2,1,0:T(8,128)}), f32[3,3,3,32,64]{4,3,2,1,0:T(8,128)}) %all-reduce.3.cloned.1.call-update) | async-done | bytes 221200 | tf_op jit(solution)/shard_map/psum | solution.py:83
  775.9 51.3 %reduce-scatter.4.cloned.1.call-done = f32[16,4096]{1,0:T(8,128)} async-done(((f32[128,4096]{1,0:T(8,128)}), f32[16,4096]{1,0:T(8,128)}) %reduce-scatter.4.cloned.1.call-update) | async-done | bytes 262160
  (57 shorter events, 46.0 us)
Async XLA Ops:
  7.2 170.2 %copy-start = (bf16[3,3,3,32,64]{4,3,2,1,0:T(8,128)(2,1)S(1)}, bf16[3,3,3,32,64]{4,3,2,1,0:T(8,128)(2,1)}, u32[]{:S(2)}) copy-start(bf16[3,3,3,32,64]{4,3,2,1,0:T(8,128)(2,1)} %param.5) | copy-start | bytes 331780
  14.2 35.5 %collective-permute-start = (bf16[1,1,64,64,32]{3,4,2,1,0:T(8,128)(2,1)S(1)}, bf16[1,1,64,64,32]{3,4,2,1,0:T(8,128)(2,1)S(1)}, u32[]{:S(2)}, u32[]{:S(2)}) collective-permute-start(bf16[1,1,64,64,32]{3,4,2,1,0:T(8,128)(2,1)S(1)} %copy.125), channel_id=1, source_target_pairs={{0,16},{16,32},{32,48},{48,64},{64,80},{80,96},{96,112},{1,17},{17... | collective-permute-start | bytes 786440 | tf_op jit(solution)/shard_map/ppermute | solution.py:13
  175.0 2.4 copy-start.6
  195.8 10.1 %copy-start.3 = (f32[4,32,8,5,64]{4,2,3,1,0:T(8,128)S(1)}, f32[4,32,8,5,64]{4,2,3,1,0:T(8,128)}, u32[]{:S(2)}) copy-start(f32[4,32,8,5,64]{4,2,3,1,0:T(8,128)} %get-tuple-element.18) | copy-start | bytes 3932164
  195.8 15.0 %all-to-all-start = ((bf16[8,2,16384]{2,1,0:T(2,128)(2,1)}), bf16[8,2,16384]{2,1,0:T(2,128)(2,1)S(1)}, u32[]{:S(2)}, u32[]{:S(2)}) async-start(bf16[8,2,16384]{2,1,0:T(2,128)(2,1)} %reshape.71), calls=%async_computation | async-start | bytes 1048576 | tf_op jit(solution)/shard_map/all_to_all | solution.py:71
  202.0 174.8 %all-gather.2.cloned.1.call-start = ((), (), s32[]{:S(2)}) async-start(), calls=%async_computation.3 | async-start | bytes 9437184 | tf_op jit(solution)/shard_map/all_gather | solution.py:77
  237.2 3.4 copy-start.5
  237.2 3.5 copy-start.7
  402.2 13.6 %copy-start.4 = (pred[8,6]{1,0:T(8,128)(4,1)S(1)}, pred[8,6]{1,0:T(8,128)(4,1)}, u32[]{:S(2)}) copy-start(pred[8,6]{1,0:T(8,128)(4,1)} %constant.31) | copy-start | bytes 148
  419.7 70.3 %all-to-all-start.1 = ((bf16[8,2,16384]{2,1,0:T(2,128)(2,1)}), bf16[8,2,16384]{2,1,0:T(2,128)(2,1)S(1)}, u32[]{:S(2)}, u32[]{:S(2)}) async-start(bf16[8,2,16384]{2,1,0:T(2,128)(2,1)} %reshape.73), calls=%async_computation.1 | async-start | bytes 1048576 | tf_op jit(solution)/shard_map/all_to_all | solution.py:80
  424.6 200.6 %all-reduce.5.cloned.1.call-start = ((), (), s32[]{:S(2)}) async-start(), calls=%async_computation.5 | async-start | bytes 221184 | tf_op jit(solution)/shard_map/psum | solution.py:84
  489.9 284.1 %all-reduce.3.cloned.1.call-start = ((), (), s32[]{:S(2)}) async-start(), calls=%async_computation.4 | async-start | bytes 884736 | tf_op jit(solution)/shard_map/psum | solution.py:83
  502.3 46.7 %copy-start.2 = (f32[16,16,8,3,128]{4,1,3,2,0:T(8,128)S(1)}, f32[16,16,8,3,128]{4,1,3,2,0:T(8,128)}, u32[]{:S(2)}) copy-start(f32[16,16,8,3,128]{4,1,3,2,0:T(8,128)} %copy.139) | copy-start | bytes 9437188
  548.9 278.3 %reduce-scatter.4.cloned.1.call-start = ((), (), s32[]{:S(2)}) async-start(), calls=%async_computation.6 | async-start | bytes 2359296
  625.2 206.2 %copy-start.1 = (bf16[3,3,3,32,64]{4,3,2,1,0:T(8,128)(2,1)S(1)}, bf16[3,3,3,32,64]{4,3,2,1,0:T(8,128)(2,1)}, u32[]{:S(2)}) copy-start(bf16[3,3,3,32,64]{4,3,2,1,0:T(8,128)(2,1)} %param.5) | copy-start | bytes 331780
Sparse Core Ops, SparseCore 0:
  206.0 170.6 all-gather.1
  490.1 135.0 all-reduce.4
  631.2 142.7 all-reduce.2
  776.3 50.8 reduce-scatter.3
where the time goes:
time: 853 us; the launch traced here: 838 us
  waiting for transfers between devices  343 us (40%)
  local copies, waits for them, and re-layouts  263 us (31%)
  matrix products  137 us (16%)
  other arithmetic  66 us (8%)
  starting transfers between devices  15.2 us (2%)
  between operations  14.4 us (2%)
    psum x1, waiting for transfers between devices, shards(): total_a = lax.psum(local_a, ('mp', 'dp'))  147 us
    transpose x2, matrix products, kernel_grad(): return jnp.transpose(result, (1, 2, 3, 0, 4))  98.3 us
    all_gather x1, waiting for transfers between devices, shards(): upstream = lax.all_gather(cotangent, 'mp', axis=4, tiled=True)  97.7 us
    unnamed x32, local copies, waits for them, and re-layouts  66.3 us
    concatenate x1, other arithmetic, shards(): padded_x = pad_sides(jnp.concatenate([below, field], axis=1))  58.2 us
    unnamed x5, waiting for transfers between devices  51.4 us
    psum x1, waiting for transfers between devices, shards(): total_b = lax.psum(local_b, 'dp')  45.1 us
    concatenate x2, local copies, waits for them, and re-layouts, shards(): padded_x = pad_sides(jnp.concatenate([below, field], axis=1))  39.5 us
  transfers between devices with their start and end apart: 7, of which 5 were waited for; matrix products, arithmetic and copies ran while one was open for 32% of the time, Pallas kernels for 0%

commit v1 on v0

--- a/solution.py
+++ b/solution.py
@@ -80,7 +80,9 @@
     back = lax.all_to_all(back_group, "mp", split_axis=1, concat_axis=4, tiled=True)
     delta = (back.astype(jnp.float32) * jnp.where(pre > 0, 1.0, 0.3)).astype(jnp.bfloat16)
     local_a = kernel_grad(padded_x, delta)
-    total_a = lax.psum(local_a, ("mp", "dp"))
+    total_a = local_a
+    for mesh_axis in ("mp", "dp"):
+        total_a = lax.psum(total_a, mesh_axis)
     total_b = lax.psum(local_b, "dp")
     samples_all = samp_local * lax.axis_size("dp")
     grad_a = total_a / math.sqrt(samples_all * (GRID // 2) ** 3)

time: 853 us -> 685 us (0.80)
  waiting for transfers between devices: 343 us -> 174 us
    all_gather x1, waiting for transfers between devices: 97.7 us -> 0.01 us  [shards(): upstream = lax.all_gather(cotangent, 'mp', axis=4, tiled=True)]
    psum x2, waiting for transfers between devices: 192 us -> 122 us  [shards(): total_a = lax.psum(total_a, mesh_axis)]
    unnamed x32 -> x34, local copies, waits for them, and re-layouts: 66.3 us -> 66 us
  transfers between devices with their start and end apart: 7 -> 7, of which waited for: 5 -> 3; matrix products, arithmetic and copies ran while one was open for 32% -> 59% of each run, Pallas kernels for 0% -> 0%
where the time goes in v1:
time: 685 us; the launch traced here: 672 us
  local copies, waits for them, and re-layouts  265 us (39%)
  waiting for transfers between devices  174 us (25%)
  matrix products  138 us (20%)
  other arithmetic  66.1 us (10%)
  starting transfers between devices  15.3 us (2%)
  between operations  14.3 us (2%)
    psum x2, waiting for transfers between devices, shards(): total_a = lax.psum(total_a, mesh_axis)  122 us
    transpose x2, matrix products, kernel_grad(): return jnp.transpose(result, (1, 2, 3, 0, 4))  98.8 us
    unnamed x34, local copies, waits for them, and re-layouts  66 us
    concatenate x1, other arithmetic, shards(): padded_x = pad_sides(jnp.concatenate([below, field], axis=1))  58.2 us
    unnamed x5, waiting for transfers between devices  51.5 us
    concatenate x2, local copies, waits for them, and re-layouts, shards(): padded_x = pad_sides(jnp.concatenate([below, field], axis=1))  39.6 us
    conv_general_dilated x6, local copies, waits for them, and re-layouts, forward_conv(): lax.conv_general_dilated(padded, kernel, (2, 2, 2), 'VALID', dimension_nu...  37.1 us
    all_to_all x4, local copies, waits for them, and re-layouts, shards(): lax.all_to_all(hidden, 'mp', split_axis=4, concat_axis=1, tiled=True)  33.1 us
  transfers between devices with their start and end apart: 7, of which 3 were waited for; matrix products, arithmetic and copies ran while one was open for 59% of the time, Pallas kernels for 0%

profile of v1, /device:TPU:1, one launch (start us, length us, event | category | flops | bytes accessed | tf_op | source)
XLA Modules:
  0.0 671.9 jit_solution(3457501782090073605)
XLA Ops:
  7.2 4.9 copy.124
  14.3 4.0 collective-permute-start
  20.9 31.5 %copy.127 = bf16[1,8,64,64,32]{4,0,3,2,1:T(2,128)(2,1)} copy(bf16[1,8,64,64,32]{2,4,3,1,0:T(8,128)(2,1)} %bitcast.69) | data formatting | bytes 4194304 | tf_op jit(solution)/shard_map/reshape | solution.py:66
  55.0 58.2 %pad_maximum_fusion = bf16[1,9,64,64,32]{4,0,3,2,1:T(2,128)(2,1)} fusion(bf16[1,8,64,64,32]{4,0,3,2,1:T(2,128)(2,1)} %copy.127, bf16[1,1,64,64,32]{4,0,3,2,1:T(2,128)(2,1)S(1)} %copy.126), kind=kLoop, calls=%fused_computation.4 | loop fusion | flops 1179648 | bytes 4718592 | tf_op jit(solution)/shard_map/concatenate | solution.py:68
  113.2 33.5 %copy.128 = bf16[1,9,64,64,32]{3,4,2,1,0:T(8,128)(2,1)} copy(bf16[1,9,64,64,32]{4,0,3,2,1:T(2,128)(2,1)} %pad_maximum_fusion) | data formatting | bytes 4718592 | tf_op jit(solution)/shard_map/concatenate | solution.py:68
  146.7 9.2 %copy.159 = bf16[9,64,1,64,32]{1,4,3,0,2:T(8,128)(2,1)} copy(bf16[9,64,1,64,32]{3,4,2,1,0:T(8,128)(2,1)} %bitcast.72) | data formatting | bytes 4718592
  156.0 6.1 pad.4.clone
  162.0 15.6 %copy.131 = bf16[9,64,1,8,10,32]{5,3,4,1,0,2:T(8,128)(2,1)} copy(bf16[9,64,1,8,10,32]{1,5,4,3,0,2:T(8,128)(2,1)} %bitcast.67) | data formatting | bytes 5898240 | tf_op jit(solution)/shard_map/conv_general_dilated | solution.py:17
  180.1 12.0 %compare_select_fusion = (f32[4,32,8,5,64]{4,2,3,1,0:T(8,128)}, bf16[4,32,8,5,64]{4,2,3,1,0:T(8,128)(2,1)S(1)}) fusion(pred[8,5]{0,1:T(8,128)(4,1)S(1)} %copy-done.7, bf16[3,3,3,32,64]{4,3,2,1,0:T(8,128)(2,1)S(1)} %copy-done, bf16[9,64,1,7,2,32]{5,3,4,1,0,2:T(8,128)(2,1)S(1)} %slice.12, bf16[9,64,1,8,10,32]{5,3,4,1,0,2:T(8,128)(2,1)} %copy.131), kind=kOutput, calls=%fused_computation.20 | convolution fusion | flops 572915712 | bytes 5541928 | tf_op jit(solution)/shard_map/conv_general_dilated | solution.py:17
  192.5 3.4 copy.133
  198.6 5.9 all-to-all-start
  204.5 10.0 %copy.141 = bf16[1,16,16,16,128]{4,3,2,1,0:T(8,128)(2,1)S(1)} copy(bf16[1,16,16,16,128]{3,2,1,0,4:T(8,128)(2,1)} %all-gather.2.cloned.1.call-done) | data formatting | bytes 2097152 | tf_op jit(solution)/shard_map/all_gather | solution.py:77
  215.7 14.0 %fusion.17 = bf16[32,32,8,6,8]{4,2,3,1,0:T(8,128)(2,1)} fusion(bf16[3,3,3,8,128]{4,3,2,1,0:T(8,128)(2,1)S(1)} %copy-done.5, bf16[16,16,1,7,1,128]{5,3,4,1,0,2:T(8,128)(2,1)S(1)} %slice.16, bf16[16,16,1,8,3,128]{5,3,4,1,0,2:T(8,128)(2,1)S(1)} %copy.144), kind=kOutput, calls=%fused_computation.24 | convolution fusion | flops 332021760 | bytes 2873344 | tf_op jit(solution)/shard_map/conv_general_dilated | solution.py:42
  229.7 13.6 %copy.145 = bf16[32,32,8,6,8]{1,4,3,2,0:T(8,128)(2,1)S(1)} copy(bf16[32,32,8,6,8]{4,2,3,1,0:T(8,128)(2,1)} %fusion.17) | data formatting | bytes 1572864 | tf_op jit(solution)/shard_map/conv_general_dilated | solution.py:42
  247.2 5.1 all-to-all-start.1
  266.0 3.4 copy.160
  269.4 4.0 pad.6.clone
  273.5 12.8 %copy.138 = bf16[32,32,1,8,6,8]{5,3,4,1,0,2:T(8,128)(2,1)} copy(bf16[32,32,1,8,6,8]{1,5,4,3,0,2:T(8,128)(2,1)} %bitcast.73) | data formatting | bytes 1572864 | tf_op jit(solution)/shard_map/conv_general_dilated | solution.py:17
  286.2 5.6 slice.14
  291.9 24.0 %copy.153 = bf16[1,32,32,32,8]{4,0,3,2,1:T(2,128)(2,1)} copy(bf16[1,32,32,32,8]{3,4,2,1,0:T(8,128)(2,1)S(1)} %bitcast.71) | data formatting | bytes 1048576 | tf_op jit(solution)/shard_map/all_to_all | solution.py:71
  315.9 14.3 %copy.154 = bf16[1,16,16,16,128]{4,0,3,2,1:T(2,128)(2,1)} copy(bf16[1,16,16,16,128]{3,2,1,0,4:T(8,128)(2,1)} %all-gather.2.cloned.1.call-done) | data formatting | bytes 2097152 | tf_op jit(solution)/shard_map/all_gather | solution.py:77
  331.2 3.4 copy.147
  334.6 3.5 fusion.12
  338.1 4.1 copy.151
  342.2 47.0 %fusion.35 = f32[3,3,3,32,64]{4,3,2,1,0:T(8,128)} fusion(bf16[1,9,64,64,32]{4,0,3,2,1:T(2,128)(2,1)} %pad_maximum_fusion, bf16[1,4,32,32,64]{4,0,3,2,1:T(2,128)(2,1)} %copy.151), kind=kOutput, calls=%fused_computation.45 | convolution fusion | flops 443596800 | bytes 3104768 | tf_op jit(solution)/shard_map/transpose | solution.py:37
  389.4 51.8 %fusion.36 = f32[3,3,3,8,128]{4,3,2,1,0:T(8,128)} fusion(bf16[1,32,32,32,8]{4,0,3,2,1:T(2,128)(2,1)} %copy.153, bf16[1,16,16,16,128]{4,0,3,2,1:T(2,128)(2,1)S(1)} %copy-done.2), kind=kOutput, calls=%fused_computation.46 | convolution fusion | flops 212629504 | bytes 1683456 | tf_op jit(solution)/shard_map/transpose | solution.py:37
  441.1 22.3 %all-reduce.4.cloned.1.call-done = f32[3,3,3,32,64]{4,3,2,1,0:T(8,128)} async-done(((f32[3,3,3,32,64]{4,3,2,1,0:T(8,128)}), f32[3,3,3,32,64]{4,3,2,1,0:T(8,128)}) %all-reduce.4.cloned.1.call-update) | async-done | bytes 221200 | tf_op jit(solution)/shard_map/psum | solution.py:85
  463.5 13.0 %broadcast_select_fusion = f32[16,16,8,3,128]{4,2,3,1,0:T(8,128)S(1)} fusion(pred[8,3]{0,1:T(4,128)(4,1)S(1)} %copy-done.8, bf16[3,3,3,8,128]{4,3,2,1,0:T(8,128)(2,1)S(1)} %copy-done.6, bf16[32,32,1,7,2,8]{5,3,4,1,0,2:T(8,128)(2,1)} %slice.14, bf16[32,32,1,8,6,8]{5,3,4,1,0,2:T(8,128)(2,1)} %copy.138), kind=kOutput, calls=%fused_computation.30 | convolution fusion | flops 329662464 | bytes 4216856 | tf_op jit(solution)/shard_map/conv_general_dilated | solution.py:17
  477.2 13.5 %copy.156 = f32[1,16,16,16,128]{2,3,1,0,4:T(8,128)} copy(f32[1,16,16,16,128]{4,2,3,1,0:T(8,128)S(1)} %slice_bitcast_fusion.1) | data formatting | bytes 4194304
  490.7 15.3 %reshape.69 = f32[128,4096]{1,0:T(8,128)} reshape(f32[128,1,16,16,16]{4,3,2,1,0:T(8,128)} %bitcast.66) | data formatting | bytes 4194304
  506.0 100.2 %all-reduce.6.cloned.1.call-done = (f32[3,3,3,32,64]{4,3,2,1,0:T(8,128)}, f32[3,3,3,8,128]{4,3,2,1,0:T(8,128)}) async-done(((f32[3,3,3,32,64]{4,3,2,1,0:T(8,128)}, f32[3,3,3,8,128]{4,3,2,1,0:T(8,128)}), (f32[3,3,3,32,64]{4,3,2,1,0:T(8,128)}, f32[3,3,3,8,128]{4,3,2,1,0:T(8,128)})) %all-reduce.6.cloned.1.call-update) | async-done | bytes 331792 | tf_op jit(solution)/shard_map/psum | solution.py:85
  609.6 51.4 %reduce-scatter.4.cloned.1.call-done = f32[16,4096]{1,0:T(8,128)} async-done(((f32[128,4096]{1,0:T(8,128)}), f32[16,4096]{1,0:T(8,128)}) %reduce-scatter.4.cloned.1.call-update) | async-done | bytes 262160
  (59 shorter events, 41.1 us)
Async XLA Ops:
  7.2 172.9 %copy-start = (bf16[3,3,3,32,64]{4,3,2,1,0:T(8,128)(2,1)S(1)}, bf16[3,3,3,32,64]{4,3,2,1,0:T(8,128)(2,1)}, u32[]{:S(2)}) copy-start(bf16[3,3,3,32,64]{4,3,2,1,0:T(8,128)(2,1)} %param.5) | copy-start | bytes 331780
  7.2 11.1 %copy-start.3 = (bf16[1,16,16,16,16]{4,3,2,1,0:T(8,128)(2,1)S(1)}, bf16[1,16,16,16,16]{4,3,2,1,0:T(8,128)(2,1)}, u32[]{:S(2)}) copy-start(bf16[1,16,16,16,16]{4,3,2,1,0:T(8,128)(2,1)} %param.7) | copy-start | bytes 393220
  7.2 197.3 %all-gather.2.cloned.1.call-start = ((), (), s32[]{:S(2)}) async-start(), calls=%async_computation.3 | async-start | bytes 9437184 | tf_op jit(solution)/shard_map/all_gather | solution.py:77
  14.3 38.1 %collective-permute-start = (bf16[1,1,64,64,32]{3,4,2,1,0:T(8,128)(2,1)S(1)}, bf16[1,1,64,64,32]{3,4,2,1,0:T(8,128)(2,1)S(1)}, u32[]{:S(2)}, u32[]{:S(2)}) collective-permute-start(bf16[1,1,64,64,32]{3,4,2,1,0:T(8,128)(2,1)S(1)} %copy.125), channel_id=1, source_target_pairs={{0,16},{16,32},{32,48},{48,64},{64,80},{80,96},{96,112},{1,17},{17... | collective-permute-start | bytes 786440 | tf_op jit(solution)/shard_map/ppermute | solution.py:13
  177.7 2.4 copy-start.7
  198.6 48.6 %all-to-all-start = ((bf16[8,2,16384]{2,1,0:T(2,128)(2,1)}), bf16[8,2,16384]{2,1,0:T(2,128)(2,1)}, u32[]{:S(2)}, u32[]{:S(2)}) async-start(bf16[8,2,16384]{2,1,0:T(2,128)(2,1)} %reshape.71), calls=%async_computation | async-start | bytes 1048576 | tf_op jit(solution)/shard_map/all_to_all | solution.py:71
  214.8 0.9 copy-start.5
  229.7 13.6 %copy-start.4 = (pred[8,6]{1,0:T(8,128)(4,1)S(1)}, pred[8,6]{1,0:T(8,128)(4,1)}, u32[]{:S(2)}) copy-start(pred[8,6]{1,0:T(8,128)(4,1)} %constant.31) | copy-start | bytes 148
  247.2 83.0 %all-to-all-start.1 = ((bf16[8,2,16384]{2,1,0:T(2,128)(2,1)}), bf16[8,2,16384]{2,1,0:T(2,128)(2,1)S(1)}, u32[]{:S(2)}, u32[]{:S(2)}) async-start(bf16[8,2,16384]{2,1,0:T(2,128)(2,1)} %reshape.73), calls=%async_computation.1 | async-start | bytes 1048576 | tf_op jit(solution)/shard_map/all_to_all | solution.py:80
  252.3 211.1 %all-reduce.4.cloned.1.call-start = ((), (), s32[]{:S(2)}) async-start(), calls=%async_computation.4 | async-start | bytes 884736 | tf_op jit(solution)/shard_map/psum | solution.py:85
  342.2 47.1 %copy-start.2 = (bf16[1,16,16,16,128]{4,0,3,2,1:T(2,128)(2,1)S(1)}, bf16[1,16,16,16,128]{4,0,3,2,1:T(2,128)(2,1)}, u32[]{:S(2)}) copy-start(bf16[1,16,16,16,128]{4,0,3,2,1:T(2,128)(2,1)} %copy.154) | copy-start | bytes 3145732
  389.3 74.2 %copy-start.6 = (bf16[3,3,3,8,128]{4,3,2,1,0:T(8,128)(2,1)S(1)}, bf16[3,3,3,8,128]{4,3,2,1,0:T(8,128)(2,1)}, u32[]{:S(2)}) copy-start(bf16[3,3,3,8,128]{4,3,2,1,0:T(8,128)(2,1)} %param.6) | copy-start | bytes 165892
  389.3 74.2 %copy-start.8 = (pred[8,3]{0,1:T(4,128)(4,1)S(1)}, pred[8,3]{0,1:T(4,128)(4,1)}, u32[]{:S(2)}) copy-start(pred[8,3]{0,1:T(4,128)(4,1)} %constant.29) | copy-start | bytes 76
  389.3 216.9 %all-reduce.6.cloned.1.call-start = ((), (), s32[]{:S(2)}) async-start(), calls=%async_computation.6 | async-start | bytes 1105920 | tf_op jit(solution)/shard_map/psum | solution.py:85
  463.4 197.6 %reduce-scatter.4.cloned.1.call-start = ((), (), s32[]{:S(2)}) async-start(), calls=%async_computation.5 | async-start | bytes 2359296
  607.7 57.5 %copy-start.1 = (bf16[3,3,3,32,64]{4,3,2,1,0:T(8,128)(2,1)S(1)}, bf16[3,3,3,32,64]{4,3,2,1,0:T(8,128)(2,1)}, u32[]{:S(2)}) copy-start(bf16[3,3,3,32,64]{4,3,2,1,0:T(8,128)(2,1)} %param.5) | copy-start | bytes 331780
Sparse Core Ops, SparseCore 0:
  21.0 170.8 all-gather.1
  389.4 73.9 all-reduce.3
  466.7 139.4 all-reduce.5
  608.5 52.5 reduce-scatter.3
